TPU v7x, 256 devices: a whole 4x4x8 slice. The times are simulated.
256 devices in a mesh: patch: 128 (over y, z, x), scene: 2 (over core).
Axes of the slice: x: 4, y: 4, z: 8, core: 2. Of those that a mesh axis runs over, the one named last changes fastest.
Arguments:
- query_rows: bfloat16 [131072, 512], P(('scene', 'patch')), parts along dimension 0, may hold values from -6.2 to 6.2
- key_rows: bfloat16 [131072, 512], P(('scene', 'patch')), parts along dimension 0, may hold values from -6.2 to 6.2
- value_rows: bfloat16 [131072, 512], P(('scene', 'patch')), parts along dimension 0, may hold values from -6 to 6
- grad_output: bfloat16 [131072, 512], P(('scene', 'patch')), parts along dimension 0, may hold values from -6 to 6
- neighbours: int32 [2048, 16], P(('scene', 'patch')), parts along dimension 0, may hold values from 0 to 1023, as said below
- owner: int32 [2048], P('scene'), parts along dimension 0, may hold values from 0 to 1023, as said below
Outputs:
- grad_query: bfloat16 [131072, 512], P(('scene', 'patch')), parts along dimension 0
- grad_key: bfloat16 [131072, 512], P(('scene', 'patch')), parts along dimension 0
- grad_value: bfloat16 [131072, 512], P(('scene', 'patch')), parts along dimension 0
There are 2 independent parts, one for each index of `scene`. A program takes and returns all parts, laid end to end along the dimension named above; each array names one. Nothing has to cross between parts.
Inputs may be any that keep to these rules, and one draw needn't show every extreme that they name: `neighbours`: each row names 16 different patch ids; the query's own patch is among them, and every one is held (through owner) by the query's device or one of the two devices beside it along patch. `owner`: A permutation; each patch id is held by a slot of the device of slots id // 8 * 8 to that plus 8 - 1.
All inputs are finite; a program needn't handle non-finite values.
Results may differ from a plain program's by a relative error of at most 0.011.
Values may be sent and summed in bfloat16 or wider, within the bound.
A program may use at most 128 MiB of HBM per device.

v0:
```python
import math

import jax
import jax.numpy as jnp
from jax import lax
from jax.sharding import PartitionSpec as P

HEADS = 8


def with_halo(block, sides, width):
    for axis, dim in sides:
        count = lax.axis_size(axis)
        forward = [(i, i + 1) for i in range(count - 1)]
        backward = [(target, source) for source, target in forward]
        low = lax.ppermute(
            lax.slice_in_dim(block, block.shape[dim] - width, None, axis=dim), axis, forward
        )
        high = lax.ppermute(lax.slice_in_dim(block, 0, width, axis=dim), axis, backward)
        block = jnp.concatenate([low, block, high], axis=dim)
    return block


def passed_along(block, axis, distance):
    devices = range(lax.axis_size(axis))
    route = [(i - distance, i) for i in devices if i - distance in devices]
    return lax.ppermute(block, axis, route)


def contract_first(left, right):
    return lax.dot_general(
        left, right, (((0,), (0,)), ((), ())), preferred_element_type=jnp.float32
    )


def contract_last(left, right):
    return lax.dot_general(
        left, right, (((1,), (1,)), ((), ())), preferred_element_type=jnp.float32
    )


def head_pass(query_h, grad_h, key_h, value_h, mask, scaling):
    scores = contract_first(query_h, key_h) * scaling
    scores = jnp.where(mask, scores, -jnp.inf)
    peak = jnp.max(scores, axis=1, keepdims=True)
    log_total = peak + jnp.log(jnp.sum(jnp.exp(scores - peak), axis=1, keepdims=True))
    weights = jnp.exp(scores - log_total)
    weights_low = weights.astype(jnp.bfloat16)
    output = contract_last(value_h, weights_low)
    delta = jnp.sum(grad_h.astype(jnp.float32) * output, axis=0)
    dweights = contract_first(grad_h, value_h)
    dscores = weights * (dweights - delta[:, None])
    dscores_low = dscores.astype(jnp.bfloat16)
    grad_q = contract_last(key_h, dscores_low) * scaling
    part_keys = jnp.dot(query_h, dscores_low, preferred_element_type=jnp.float32) * scaling
    part_values = jnp.dot(grad_h, weights_low, preferred_element_type=jnp.float32)
    return (grad_q, jnp.stack([part_keys, part_values]), jnp.stack([log_total[:, 0], delta]))


def body(query_rows, key_rows, value_rows, grad_output, neighbours, owner):
    row_count, features = query_rows.shape
    per_device = neighbours.shape[0]
    patch_rows = row_count // per_device
    head_size = features // HEADS
    scaling = 1.0 / math.sqrt(head_size)

    def heads_last(rows_in):
        return jnp.transpose(rows_in.reshape(row_count, HEADS, head_size), (1, 2, 0))

    query_t = heads_last(query_rows)
    grad_t = heads_last(grad_output)
    stacked = jnp.stack([heads_last(key_rows), heads_last(value_rows)])
    widened = with_halo(stacked, (("patch", 3),), row_count)
    device = lax.axis_index("patch")
    local_slots = owner[neighbours] - (device - 1) * per_device
    slot_mask = jnp.any(
        local_slots[:, :, None] == jnp.arange(3 * per_device, dtype=jnp.int32)[None, None, :],
        axis=1,
    )
    row_mask = jnp.repeat(jnp.repeat(slot_mask, patch_rows, axis=0), patch_rows, axis=1)

    def one_head(carry, inputs):
        query_h, grad_h, key_h, value_h = inputs
        return (carry, head_pass(query_h, grad_h, key_h, value_h, row_mask, scaling))

    unused, results = lax.scan(one_head, None, (query_t, grad_t, widened[0], widened[1]))
    grad_q_all, terms, stats = results
    from_left = passed_along(terms[..., 2 * row_count :].astype(jnp.bfloat16), "patch", 1).astype(
        jnp.float32
    )
    from_right = passed_along(terms[..., :row_count].astype(jnp.bfloat16), "patch", -1).astype(
        jnp.float32
    )
    collected = terms[..., row_count : 2 * row_count] + from_left + from_right
    grad_query = (
        jnp.transpose(grad_q_all, (2, 0, 1)).reshape(row_count, features).astype(jnp.bfloat16)
    )
    gathered = jnp.transpose(collected, (1, 3, 0, 2)).reshape(2, row_count, features)
    return (grad_query, gathered[0].astype(jnp.bfloat16), gathered[1].astype(jnp.bfloat16))


def solution(mesh):
    placed = (
        P(("scene", "patch"), None),
        P(("scene", "patch"), None),
        P(("scene", "patch"), None),
        P(("scene", "patch"), None),
        P(("scene", "patch"), None),
        P("scene"),
    )
    return jax.shard_map(
        body,
        mesh=mesh,
        in_specs=placed,
        out_specs=(
            P(("scene", "patch"), None),
            P(("scene", "patch"), None),
            P(("scene", "patch"), None),
        ),
        check_vma=False,
    )
```

profile of v0, /device:TPU:24, one launch (start us, length us, event | category | flops | bytes accessed | tf_op | source)
XLA Modules:
  0.0 177.6 jit_solution(16966640055073222472)
XLA Ops:
  0.7 1.3 copy.27
  1.9 1.3 copy.28
  3.3 10.1 %collective-permute-start.1 = (bf16[2,8,64,512]{3,2,1,0:T(8,128)(2,1)S(1)}, bf16[2,8,64,512]{3,2,1,0:T(8,128)(2,1)S(1)}, u32[]{:S(2)}, u32[]{:S(2)}) collective-permute-start(bf16[2,8,64,512]{3,2,1,0:T(8,128)(2,1)S(1)} %pad_maximum_fusion.1), channel_id=1, source_target_pairs={{2,0},{4,2},{6,4},{8,6},{10,8},{12,10},{14,12},{16,14},{18,16},{20... | collective-permute-start | bytes 3145736 | tf_op jit(solution)/shard_map/ppermute | solution.py:19
  13.4 1.9 %collective-permute-start = (bf16[2,8,64,512]{3,2,1,0:T(8,128)(2,1)S(1)}, bf16[2,8,64,512]{3,2,1,0:T(8,128)(2,1)}, u32[]{:S(2)}, u32[]{:S(2)}) collective-permute-start(bf16[2,8,64,512]{3,2,1,0:T(8,128)(2,1)S(1)} %pad_maximum_fusion.1), channel_id=1, source_target_pairs={{0,2},{2,4},{4,6},{6,8},{8,10},{10,12},{12,14},{14,16},{16,18},{18... | collective-permute-start | bytes 3145736 | tf_op jit(solution)/shard_map/ppermute | solution.py:16
  17.0 2.0 %copy.29 = bf16[512,512]{0,1:T(8,128)(2,1)} copy(bf16[512,512]{1,0:T(8,128)(2,1)} %param.8) | data formatting | bytes 1048576 | tf_op args[0]
  19.0 2.0 %copy.30 = bf16[512,512]{0,1:T(8,128)(2,1)} copy(bf16[512,512]{1,0:T(8,128)(2,1)} %param.11) | data formatting | bytes 1048576 | tf_op args[3]
  21.1 14.7 %collective-permute-done.1 = bf16[2,8,64,512]{3,2,1,0:T(8,128)(2,1)S(1)} collective-permute-done((bf16[2,8,64,512]{3,2,1,0:T(8,128)(2,1)S(1)}, bf16[2,8,64,512]{3,2,1,0:T(8,128)(2,1)S(1)}, u32[]{:S(2)}, u32[]{:S(2)}) %collective-permute-start.1) | collective-permute-done | bytes 1048608 | tf_op jit(solution)/shard_map/ppermute | solution.py:19
  35.8 8.4 %collective-permute-done = bf16[2,8,64,512]{3,2,1,0:T(8,128)(2,1)} collective-permute-done((bf16[2,8,64,512]{3,2,1,0:T(8,128)(2,1)S(1)}, bf16[2,8,64,512]{3,2,1,0:T(8,128)(2,1)}, u32[]{:S(2)}, u32[]{:S(2)}) %collective-permute-start) | collective-permute-done | bytes 1048608 | tf_op jit(solution)/shard_map/ppermute | solution.py:16
  44.3 1.4 pad_maximum_fusion
  45.8 92.1 %while.13 = (s32[]{:T(128)}, bf16[8,64,512]{2,1,0:T(8,128)(2,1)}, f32[8,2,64,1536]{3,2,0,1:T(8,128)}, bf16[8,64,1536]{2,1,0:T(8,128)(2,1)S(1)}, bf16[8,64,512]{2...) while((s32[]{:T(128)}, bf16[8,64,512]{2,1,0:T(8,128)(2,1)}, ...), condition=%wide.region_5.6_spmd.clone, body=%wide.region_1.5_spmd.clone.sunk | while | flops 614628352 | bytes 27236464 | solution.py:86
  47.0 1.6 fusion.68
  49.2 1.6 fusion.69
  50.8 1.5 convolution_bitcast_fusion.2
  52.3 1.7 fusion.70
  53.9 1.2 fusion.72
  55.2 1.2 fusion.71
  58.5 1.6 fusion.68
  60.7 1.6 fusion.69
  62.2 1.5 convolution_bitcast_fusion.2
  63.8 1.7 fusion.70
  65.4 1.2 fusion.72
  66.7 1.2 fusion.71
  69.9 1.6 fusion.68
  72.2 1.6 fusion.69
  73.7 1.5 convolution_bitcast_fusion.2
  75.3 1.7 fusion.70
  76.9 1.2 fusion.72
  78.2 1.2 fusion.71
  81.4 1.6 fusion.68
  83.7 1.6 fusion.69
  85.2 1.5 convolution_bitcast_fusion.2
  86.8 1.7 fusion.70
  88.4 1.2 fusion.72
  89.7 1.2 fusion.71
  93.0 1.6 fusion.68
  95.2 1.6 fusion.69
  96.8 1.5 convolution_bitcast_fusion.2
  98.3 1.7 fusion.70
  100.0 1.2 fusion.72
  101.2 1.2 fusion.71
  104.5 1.6 fusion.68
  106.7 1.6 fusion.69
  108.3 1.5 convolution_bitcast_fusion.2
  109.8 1.6 fusion.70
  111.5 1.2 fusion.72
  112.7 1.2 fusion.71
  116.0 1.6 fusion.68
  118.2 1.6 fusion.69
  119.8 1.5 convolution_bitcast_fusion.2
  121.3 1.7 fusion.70
  123.0 1.2 fusion.72
  124.2 1.2 fusion.71
  127.5 1.6 fusion.68
  129.8 1.6 fusion.69
  131.3 1.5 convolution_bitcast_fusion.2
  132.9 1.7 fusion.70
  134.5 1.2 fusion.72
  135.8 1.2 fusion.71
  138.0 3.2 %convert.8 = bf16[8,2,64,1536]{3,2,0,1:T(8,128)(2,1)S(1)} convert(f32[8,2,64,1536]{3,2,0,1:T(8,128)} %get-tuple-element.47) | non-fusion elementwise | flops 1572864 | bytes 9437184 | tf_op jit(solution)/shard_map/convert.3
  142.3 1.9 %collective-permute-start.2 = (bf16[8,2,64,512]{3,2,0,1:T(8,128)(2,1)}, bf16[8,2,64,512]{3,2,0,1:T(8,128)(2,1)S(1)}, u32[]{:S(2)}, u32[]{:S(2)}) collective-permute-start(bf16[8,2,64,512]{3,2,0,1:T(8,128)(2,1)} %get-tuple-element.91), channel_id=1, source_target_pairs={{0,2},{2,4},{4,6},{6,8},{8,10},{10,12},{12,14},{14,16},{16,18},{18... | collective-permute-start | bytes 3145736 | tf_op jit(solution)/shard_map/ppermute | solution.py:27
  144.2 8.1 %collective-permute-start.3 = (bf16[8,2,64,512]{3,2,0,1:T(8,128)(2,1)S(1)}, bf16[8,2,64,512]{3,2,0,1:T(8,128)(2,1)S(1)}, u32[]{:S(2)}, u32[]{:S(2)}) collective-permute-start(bf16[8,2,64,512]{3,2,0,1:T(8,128)(2,1)S(1)} %get-tuple-element.92), channel_id=1, source_target_pairs={{2,0},{4,2},{6,4},{8,6},{10,8},{12,10},{14,12},{16,14},{18,16},{20... | collective-permute-start | bytes 3145736 | tf_op jit(solution)/shard_map/ppermute | solution.py:27
  152.4 2.0 %copy.34 = bf16[512,512]{1,0:T(8,128)(2,1)} copy(bf16[512,512]{0,1:T(8,128)(2,1)} %bitcast.112) | data formatting | bytes 1048576
  154.4 17.9 %collective-permute-done.2 = bf16[8,2,64,512]{3,2,0,1:T(8,128)(2,1)S(1)} collective-permute-done((bf16[8,2,64,512]{3,2,0,1:T(8,128)(2,1)}, bf16[8,2,64,512]{3,2,0,1:T(8,128)(2,1)S(1)}, u32[]{:S(2)}, u32[]{:S(2)}) %collective-permute-start.2) | collective-permute-done | bytes 1048608 | tf_op jit(solution)/shard_map/ppermute | solution.py:27
  173.3 2.2 %fusion.35 = bf16[2,512,8,64]{1,3,2,0:T(8,128)(2,1)S(1)} fusion(bf16[8,2,64,512]{3,2,0,1:T(8,128)(2,1)S(1)} %collective-permute-done.3, bf16[8,2,64,512]{3,2,0,1:T(8,128)(2,1)S(1)} %collective-permute-done.2, f32[8,2,64,1536]{3,2,0,1:T(8,128)} %get-tuple-element.47), kind=kLoop, calls=%fused_computation.47 | loop fusion | flops 2621440 | bytes 5242880 | tf_op jit(solution)/shard_map/convert.1
  (63 shorter events, 27.2 us)
Async XLA Ops:
  0.6 14.9 %copy-start = (s32[1024]{0:T(1024)S(1)}, s32[1024]{0:T(1024)}, u32[]{:S(2)}) copy-start(s32[1024]{0:T(1024)} %param.13) | copy-start | bytes 12292
  0.6 14.8 %copy-start.1 = (s32[8,16]{1,0:T(8,128)S(1)}, s32[8,16]{1,0:T(8,128)}, u32[]{:S(2)}) copy-start(s32[8,16]{1,0:T(8,128)} %param.12) | copy-start | bytes 1540
  3.3 32.5 %collective-permute-start.1 = (bf16[2,8,64,512]{3,2,1,0:T(8,128)(2,1)S(1)}, bf16[2,8,64,512]{3,2,1,0:T(8,128)(2,1)S(1)}, u32[]{:S(2)}, u32[]{:S(2)}) collective-permute-start(bf16[2,8,64,512]{3,2,1,0:T(8,128)(2,1)S(1)} %pad_maximum_fusion.1), channel_id=1, source_target_pairs={{2,0},{4,2},{6,4},{8,6},{10,8},{12,10},{14,12},{16,14},{18,16},{20... | collective-permute-start | bytes 3145736 | tf_op jit(solution)/shard_map/ppermute | solution.py:19
  13.4 30.8 %collective-permute-start = (bf16[2,8,64,512]{3,2,1,0:T(8,128)(2,1)S(1)}, bf16[2,8,64,512]{3,2,1,0:T(8,128)(2,1)}, u32[]{:S(2)}, u32[]{:S(2)}) collective-permute-start(bf16[2,8,64,512]{3,2,1,0:T(8,128)(2,1)S(1)} %pad_maximum_fusion.1), channel_id=1, source_target_pairs={{0,2},{2,4},{4,6},{6,8},{8,10},{10,12},{12,14},{14,16},{16,18},{18... | collective-permute-start | bytes 3145736 | tf_op jit(solution)/shard_map/ppermute | solution.py:16
  142.3 30.0 %collective-permute-start.2 = (bf16[8,2,64,512]{3,2,0,1:T(8,128)(2,1)}, bf16[8,2,64,512]{3,2,0,1:T(8,128)(2,1)S(1)}, u32[]{:S(2)}, u32[]{:S(2)}) collective-permute-start(bf16[8,2,64,512]{3,2,0,1:T(8,128)(2,1)} %get-tuple-element.91), channel_id=1, source_target_pairs={{0,2},{2,4},{4,6},{6,8},{8,10},{10,12},{12,14},{14,16},{16,18},{18... | collective-permute-start | bytes 3145736 | tf_op jit(solution)/shard_map/ppermute | solution.py:27
  144.2 29.1 %collective-permute-start.3 = (bf16[8,2,64,512]{3,2,0,1:T(8,128)(2,1)S(1)}, bf16[8,2,64,512]{3,2,0,1:T(8,128)(2,1)S(1)}, u32[]{:S(2)}, u32[]{:S(2)}) collective-permute-start(bf16[8,2,64,512]{3,2,0,1:T(8,128)(2,1)S(1)} %get-tuple-element.92), channel_id=1, source_target_pairs={{2,0},{4,2},{6,4},{8,6},{10,8},{12,10},{14,12},{16,14},{18,16},{20... | collective-permute-start | bytes 3145736 | tf_op jit(solution)/shard_map/ppermute | solution.py:27
where the time goes:
time: 180 us; the launch traced here: 178 us
  matrix products  70.7 us (39%)
  waiting for transfers between devices  42.1 us (23%)
  local copies, waits for them, and re-layouts  22.3 us (12%)
  starting transfers between devices  22.1 us (12%)
  other arithmetic  19.3 us (11%)
    dot_general x16, matrix products, contract_first(): lax.dot_general(left, right, (((0,), (0,)), ((), ())), preferred_element_...  26.3 us
    dot_general x16, matrix products, contract_last(): lax.dot_general(left, right, (((1,), (1,)), ((), ())), preferred_element_...  22.4 us
    ppermute x2, waiting for transfers between devices, passed_along(): return lax.ppermute(block, axis, route)  18.9 us
    ppermute x1, waiting for transfers between devices, with_halo(): lax.ppermute(lax.slice_in_dim(block, 0, width, axis=dim), axis, backward)  14.7 us
    dot_general x8, matrix products, head_pass(): jnp.dot(grad_h, weights_low, preferred_element_type=jnp.float32)  12.2 us
    unnamed x11, local copies, waits for them, and re-layouts  10.7 us
    ppermute x1, starting transfers between devices, with_halo(): lax.ppermute(lax.slice_in_dim(block, 0, width, axis=dim), axis, backward)  10.1 us
    ppermute x2, starting transfers between devices, passed_along(): return lax.ppermute(block, axis, route)  10 us
  transfers between devices with their start and end apart: 4, of which 4 were waited for; matrix products, arithmetic and copies ran while one was open for 4% of the time, Pallas kernels for 0%

commit v1 on v0

v1 whole, which is shorter than its diff:
```python
import functools
import math

import jax
import jax.numpy as jnp
from jax import lax
from jax.experimental import pallas as pl
from jax.experimental.pallas import tpu as pltpu
from jax.sharding import PartitionSpec as P

HEADS = 8
MESH = pl.DeviceIdType.MESH
BF16, F32 = jnp.bfloat16, jnp.float32
MASKED = -1e30
ROWS = 512
TILE = 256
PAIRS = 4
CHUNKS = PAIRS * ROWS // TILE
RING = 5
LAG_B, LAG_C, LAG_D = 2, 4, 7
AHEAD = 2


def dot(left, right):
    return lax.dot_general(left, right, (((1,), (0,)), ((), ())), preferred_element_type=F32)


def dot_last(left, right):
    return lax.dot_general(left, right, (((1,), (1,)), ((), ())), preferred_element_type=F32)


def kernel(
    n,
    query, key, value, gout, neighbours, owner,
    grad_query, grad_key, grad_value,
    own_ids, near_ids, k_pair, v_pair, k_turned, q_all, g_all, bias, hot, mask_out, mask_in,
    e_own, d_own, e_near, d_near, part_own, part_out, part_in, final_out, final_in,
    weights, dscores, dq_own, dq_out, dq_in, dq_done, dk_done, dv_done,
    load_sem, bulk_send, bulk_recv, mask_send, mask_recv, part_send, part_recv,
    final_send, final_recv, dq_send, dq_recv, store_sem,
):
    me = lax.axis_index("patch")
    target = (jnp.minimum(me + 1, n - 1), jnp.maximum(me - 1, 0))
    sends = (me < n - 1, me > 0)
    receives = (me > 0, me < n - 1)
    scaling = 1.0 / math.sqrt(64)
    base2 = scaling * math.log2(math.e)

    barrier = pltpu.get_barrier_semaphore()
    for flow in (0, 1):

        @pl.when(sends[flow])
        def _(flow=flow):
            pl.semaphore_signal(
                barrier, inc=1, device_id={"patch": target[flow]}, device_id_type=MESH
            )

    own_copy = pltpu.make_async_copy(owner, own_ids, load_sem.at[4 * PAIRS])
    near_copy = pltpu.make_async_copy(neighbours, near_ids, load_sem.at[4 * PAIRS + 1])
    own_copy.start()
    near_copy.start()

    def load(pair, array):
        lanes = pl.ds(128 * pair, 128)
        middle = pl.ds(ROWS, ROWS)
        source = (key, value, query, gout)[array].at[:, lanes]
        place = (
            k_pair.at[pair],
            v_pair.at[pair],
            q_all.at[pair, middle],
            g_all.at[pair, middle],
        )[array]
        return pltpu.make_async_copy(source, place, load_sem.at[4 * pair + array])

    for pair in range(PAIRS):
        for array in range(4):
            load(pair, array).start()

    own_copy.wait()
    near_copy.wait()
    lane = lax.broadcasted_iota(jnp.int32, (8, 128), 1)
    low_lane = lax.rem(lane, 64)
    first_id = 8 * (me - 1)
    held = [jnp.full((8, 128), -1, jnp.int32) for _ in range(3)]
    for t in range(24):
        number = first_id + t
        valid = (number >= 0) & (number < 8 * n)
        slot = own_ids[jnp.clip(number, 0, 8 * n - 1)] - first_id
        slot = jnp.where(valid, slot, -1000)
        held = [jnp.where(low_lane == slot - 8 * w, number, held[w]) for w in range(3)]
    near = near_ids[...]
    found = [jnp.zeros((8, 128), jnp.bool_) for _ in range(3)]
    for j in range(16):
        column = jnp.broadcast_to(near[:, j : j + 1], (8, 128))
        found = [found[w] | (column == held[w]) for w in range(3)]
    masks = [jnp.where(found[w] | (low_lane >= 8), 0.0, MASKED) for w in range(3)]
    mask_out[0] = masks[2]
    mask_out[1] = masks[0]

    def spread(block, mask):
        for a in range(8):
            rows = pl.ds(ROWS * block + 64 * a, 64)
            bias[rows, :] = jnp.broadcast_to(mask[a : a + 1, :], (64, 128)).astype(BF16)

    spread(1, masks[1])
    row_slot = lax.broadcasted_iota(jnp.int32, (ROWS, 128), 0) // 64
    lane_slot = lax.rem(lax.broadcasted_iota(jnp.int32, (ROWS, 128), 1), 64)
    hot[...] = jnp.where(row_slot == lane_slot, 1.0, 0.0).astype(BF16)

    for flow in (0, 1):

        @pl.when(jnp.logical_not(receives[flow]))
        def _(flow=flow):
            rows = pl.ds(2 * ROWS * flow, ROWS)
            for pair in range(PAIRS):
                q_all[pair, rows, :] = jnp.zeros((ROWS, 128), BF16)
                g_all[pair, rows, :] = jnp.zeros((ROWS, 128), BF16)
            mask_in[flow] = jnp.full((8, 128), MASKED, F32)
            part_in[flow] = jnp.full((CHUNKS, 8, TILE), MASKED, F32)
            final_in[flow] = jnp.zeros((CHUNKS, 8, TILE), F32)
            dq_in[flow] = jnp.zeros((CHUNKS, 128, TILE), BF16)

    inner = receives[0] & receives[1]

    @pl.when(inner)
    def _():
        pl.semaphore_wait(barrier, 2)

    @pl.when(jnp.logical_not(inner))
    def _():
        pl.semaphore_wait(barrier, 1)

    def remote(source, place, send_sem, recv_sem, flow):
        return pltpu.make_async_remote_copy(
            src_ref=source,
            dst_ref=place,
            send_sem=send_sem,
            recv_sem=recv_sem,
            device_id={"patch": target[flow]},
            device_id_type=MESH,
        )

    def mask_copy(flow):
        return remote(
            mask_out.at[flow], mask_in.at[flow], mask_send.at[flow], mask_recv.at[flow], flow
        )

    def split(chunk):
        pair = lax.div(chunk, 2)
        first = pl.multiple_of(lax.rem(chunk, 2) * TILE, TILE)
        return pair, first

    def bulk_copy(chunk, flow, array):
        pair, first = split(chunk)
        lanes = pl.ds(pl.multiple_of(pair * 128, 128), 128)
        source = (query, gout)[array].at[pl.ds(first, TILE), lanes]
        place = (q_all, g_all)[array].at[pair, pl.ds(2 * ROWS * flow + first, TILE)]
        at = (flow, chunk, array)
        return remote(source, place, bulk_send.at[at], bulk_recv.at[at], flow)

    def part_copy(chunk, flow):
        at = (flow, chunk)
        return remote(part_out.at[at], part_in.at[at], part_send.at[at], part_recv.at[at], flow)

    def final_copy(chunk, flow):
        at = (flow, chunk)
        return remote(
            final_out.at[chunk], final_in.at[at], final_send.at[at], final_recv.at[at], flow
        )

    def dq_copy(chunk, flow):
        at = (flow, chunk)
        return remote(dq_out.at[at], dq_in.at[at], dq_send.at[at], dq_recv.at[at], flow)

    def start(copies):
        for flow in (0, 1):

            @pl.when(sends[flow])
            def _(flow=flow):
                for copy in copies(flow):
                    copy.start()

    def wait_send(copies):
        for flow in (0, 1):

            @pl.when(sends[flow])
            def _(flow=flow):
                for copy in copies(flow):
                    copy.wait_send()

    def wait_recv(copies):
        for flow in (0, 1):

            @pl.when(receives[flow])
            def _(flow=flow):
                for copy in copies(flow):
                    copy.wait_recv()

    def bulk_copies(chunk):
        return lambda flow: [bulk_copy(chunk, flow, array) for array in (0, 1)]

    start(lambda flow: [mask_copy(flow)])
    for chunk in range(AHEAD):
        start(bulk_copies(jnp.int32(chunk)))

    for pair in range(PAIRS):
        for array in range(4):
            load(pair, array).wait()
    for pair in range(PAIRS):
        k_turned[pair] = k_pair[pair].T

    half = lax.broadcasted_iota(jnp.int32, (1, 128), 1) < 64
    halves = (half, jnp.logical_not(half))

    def keys_of(pair, h):
        return (
            jnp.where(halves[h], k_pair[pair], hot[...]),
            jnp.where(halves[h], v_pair[pair], jnp.zeros((), BF16)),
        )

    def scores_of(keys, values, pair, rows, h, e_ref, d_ref):
        queries = jnp.where(halves[h], q_all[pair, rows, :], bias[rows, :])
        scores = dot_last(keys, queries)
        peak = jnp.max(scores, axis=0, keepdims=True)
        raised = jnp.exp2((scores - peak) * base2)
        e_ref[...] = raised
        dweights = dot_last(values, g_all[pair, rows, :])
        d_ref[...] = dweights
        total = jnp.sum(raised, axis=0, keepdims=True)
        weighted = jnp.sum(raised * dweights, axis=0, keepdims=True)
        return [peak, total, weighted]

    def rows_of(found):
        return jnp.concatenate(found + [jnp.zeros((1, TILE), F32)] * (8 - len(found)), axis=0)

    def own_scores(pair, carry):
        both = [keys_of(pair, h) for h in (0, 1)]
        for t in (0, 1):
            chunk = 2 * pair + t
            found = []
            for h in (0, 1):
                rows = pl.ds(ROWS + TILE * t, TILE)
                found += scores_of(
                    *both[h], pair, rows, h, e_own.at[chunk, h], d_own.at[chunk, h]
                )
            part_own[chunk] = rows_of(found)
        return carry

    lax.fori_loop(0, PAIRS, own_scores, 0)

    wait_recv(lambda flow: [mask_copy(flow)])
    spread(0, mask_in[0])
    spread(2, mask_in[1])

    def near_scores(chunk):
        pair, first = split(chunk)
        slot = lax.rem(chunk, RING)
        found = [[], []]
        for h in (0, 1):
            keys, values = keys_of(pair, h)
            for side in (0, 1):
                rows = pl.ds(2 * ROWS * side + first, TILE)
                found[side] += scores_of(
                    keys, values, pair, rows, h, e_near.at[slot, side, h], d_near.at[slot, side, h]
                )
        part_out[1, chunk] = rows_of(found[0])
        part_out[0, chunk] = rows_of(found[1])

    def combine(chunk):
        parts = [part_own[chunk], part_in[0, chunk], part_in[1, chunk]]
        found = []
        for h in (0, 1):
            peaks, totals, sums = (
                [part[3 * h + i : 3 * h + i + 1, :] for part in parts] for i in range(3)
            )
            top = functools.reduce(jnp.maximum, peaks)
            scales = [jnp.exp2((peak - top) * base2) for peak in peaks]
            total = sum(scale * one for scale, one in zip(scales, totals))
            delta = sum(scale * one for scale, one in zip(scales, sums)) / total
            found += [top * base2 + jnp.log2(total), delta]
        final_out[chunk] = rows_of(found)

    def finish(chunk):
        pair, first = split(chunk)
        slot = lax.rem(chunk, RING)
        for h in (0, 1):
            turned = k_turned[pair, pl.ds(64 * h, 64), :]
            for block in range(3):
                side = block // 2
                if block == 1:
                    e_ref, d_ref = e_own.at[chunk, h], d_own.at[chunk, h]
                    peaks, finals = part_own.at[chunk], final_out.at[chunk]
                else:
                    e_ref, d_ref = e_near.at[slot, side, h], d_near.at[slot, side, h]
                    peaks, finals = part_out.at[1 - side, chunk], final_in.at[side, chunk]
                peak = peaks[3 * h : 3 * h + 1, :]
                log_total = finals[2 * h : 2 * h + 1, :]
                delta = finals[2 * h + 1 : 2 * h + 2, :]
                weight = e_ref[...] * jnp.exp2(peak * base2 - log_total)
                dscore = (weight * (d_ref[...] - delta)).astype(BF16)
                lanes = pl.ds(ROWS * block + first, TILE)
                weights[h, :, lanes] = weight.astype(BF16)
                dscores[h, :, lanes] = dscore
                part = dot(turned, dscore)
                if block == 1:
                    dq_own[chunk, pl.ds(64 * h, 64), :] = part
                else:
                    dq_out[1 - side, chunk, pl.ds(64 * h, 64), :] = part.astype(BF16)

    def store(which, pair):
        lanes = pl.ds(pl.multiple_of(pair * 128, 128), 128)
        source = (dk_done, dv_done)[which].at[pair]
        place = (grad_key, grad_value)[which].at[:, lanes]
        return pltpu.make_async_copy(source, place, store_sem.at[which, pair])

    def store_query(chunk):
        pair, first = split(chunk)
        lanes = pl.ds(pl.multiple_of(pair * 128, 128), 128)
        place = grad_query.at[pl.ds(first, TILE), lanes]
        return pltpu.make_async_copy(dq_done.at[chunk], place, store_sem.at[2, chunk])

    def key_gradients(pair):
        dv = [dot(weights[h], g_all[pair]) for h in (0, 1)]
        dk = [dot(dscores[h], q_all[pair]) for h in (0, 1)]
        dv_done[pair] = jnp.where(half, dv[0], dv[1]).astype(BF16)
        dk_done[pair] = (jnp.where(half, dk[0], dk[1]) * scaling).astype(BF16)

    def query_gradients(chunk):
        total = dq_own[chunk] + dq_in[0, chunk].astype(F32) + dq_in[1, chunk].astype(F32)
        dq_done[chunk] = (total * scaling).T.astype(BF16)

    def step(s, carry):
        @pl.when(s < CHUNKS)
        def _():
            wait_recv(bulk_copies(s))

            @pl.when(s + AHEAD < CHUNKS)
            def _():
                start(bulk_copies(s + AHEAD))

            near_scores(s)
            start(lambda flow: [part_copy(s, flow)])

        @pl.when((s >= LAG_B) & (s < CHUNKS + LAG_B))
        def _():
            chunk = s - LAG_B
            wait_recv(lambda flow: [part_copy(chunk, flow)])
            combine(chunk)
            start(lambda flow: [final_copy(chunk, flow)])

        @pl.when((s >= LAG_C) & (s < CHUNKS + LAG_C))
        def _():
            chunk = s - LAG_C
            wait_recv(lambda flow: [final_copy(chunk, flow)])
            finish(chunk)
            start(lambda flow: [dq_copy(chunk, flow)])

            @pl.when(lax.rem(chunk, 2) == 1)
            def _():
                pair = lax.div(chunk, 2)
                key_gradients(pair)
                store(0, pair).start()
                store(1, pair).start()

        @pl.when(s >= LAG_D)
        def _():
            chunk = s - LAG_D
            wait_recv(lambda flow: [dq_copy(chunk, flow)])
            query_gradients(chunk)
            store_query(chunk).start()

        return carry

    lax.fori_loop(0, CHUNKS + LAG_D, step, 0)

    wait_send(lambda flow: [mask_copy(flow)])

    def drain(chunk, carry):
        wait_send(
            lambda flow: [
                *bulk_copies(chunk)(flow),
                part_copy(chunk, flow),
                final_copy(chunk, flow),
                dq_copy(chunk, flow),
            ]
        )
        store_query(chunk).wait()
        return carry

    lax.fori_loop(0, CHUNKS, drain, 0)
    for pair in range(PAIRS):
        store(0, jnp.int32(pair)).wait()
        store(1, jnp.int32(pair)).wait()


def body(n, query_rows, key_rows, value_rows, grad_output, neighbours, owner):
    rows, features = query_rows.shape
    out = jax.ShapeDtypeStruct((rows, features), BF16)
    whole = pl.BlockSpec(memory_space=pl.ANY)
    dma = pltpu.SemaphoreType.DMA
    wide = ROWS * 3
    return pl.pallas_call(
        functools.partial(kernel, n),
        out_shape=[out] * 3,
        in_specs=[whole] * 6,
        out_specs=[whole] * 3,
        scratch_shapes=[
            pltpu.SMEM(owner.shape, jnp.int32),
            pltpu.VMEM(neighbours.shape, jnp.int32),
            pltpu.VMEM((PAIRS, ROWS, 128), BF16),
            pltpu.VMEM((PAIRS, ROWS, 128), BF16),
            pltpu.VMEM((PAIRS, 128, ROWS), BF16),
            pltpu.VMEM((PAIRS, wide, 128), BF16),
            pltpu.VMEM((PAIRS, wide, 128), BF16),
            pltpu.VMEM((wide, 128), BF16),
            pltpu.VMEM((ROWS, 128), BF16),
            pltpu.VMEM((2, 8, 128), F32),
            pltpu.VMEM((2, 8, 128), F32),
            pltpu.VMEM((CHUNKS, 2, ROWS, TILE), F32),
            pltpu.VMEM((CHUNKS, 2, ROWS, TILE), F32),
            pltpu.VMEM((RING, 2, 2, ROWS, TILE), F32),
            pltpu.VMEM((RING, 2, 2, ROWS, TILE), F32),
            pltpu.VMEM((CHUNKS, 8, TILE), F32),
            pltpu.VMEM((2, CHUNKS, 8, TILE), F32),
            pltpu.VMEM((2, CHUNKS, 8, TILE), F32),
            pltpu.VMEM((CHUNKS, 8, TILE), F32),
            pltpu.VMEM((2, CHUNKS, 8, TILE), F32),
            pltpu.VMEM((2, ROWS, wide), BF16),
            pltpu.VMEM((2, ROWS, wide), BF16),
            pltpu.VMEM((CHUNKS, 128, TILE), F32),
            pltpu.VMEM((2, CHUNKS, 128, TILE), BF16),
            pltpu.VMEM((2, CHUNKS, 128, TILE), BF16),
            pltpu.VMEM((CHUNKS, TILE, 128), BF16),
            pltpu.VMEM((PAIRS, ROWS, 128), BF16),
            pltpu.VMEM((PAIRS, ROWS, 128), BF16),
            dma((4 * PAIRS + 2,)),
            dma((2, CHUNKS, 2)),
            dma((2, CHUNKS, 2)),
            dma((2,)),
            dma((2,)),
            dma((2, CHUNKS)),
            dma((2, CHUNKS)),
            dma((2, CHUNKS)),
            dma((2, CHUNKS)),
            dma((2, CHUNKS)),
            dma((2, CHUNKS)),
            dma((3, CHUNKS)),
        ],
        compiler_params=pltpu.CompilerParams(
            collective_id=0, has_side_effects=True, vmem_limit_bytes=60 << 20
        ),
    )(query_rows, key_rows, value_rows, grad_output, neighbours, owner)


def solution(mesh):
    split = P(("scene", "patch"), None)
    return jax.shard_map(
        functools.partial(body, mesh.shape["patch"]),
        mesh=mesh,
        in_specs=(split, split, split, split, split, P("scene")),
        out_specs=(split, split, split),
        check_vma=False,
    )
```

time: 180 us -> 66.4 us (0.37); the launches traced: 178 us -> 66.3 us
  matrix products: 70.7 us -> 0 us
  Pallas kernels: 0 us -> 61.6 us
  waiting for transfers between devices: 42.1 us -> 0 us
  starting transfers between devices: 22.1 us -> 0 us
  other arithmetic: 19.3 us -> 0 us
  local copies, waits for them, and re-layouts: 22.3 us -> 3.95 us
    dot_general x48 -> x0, matrix products: 70.7 us -> none  [the longest x16 26.3 us: contract_first(): lax.dot_general(left, right, (((0,), (0,)), ((), ())), preferred_element_...]
    pallas_call x0 -> x1, Pallas kernels: none -> 61.6 us  [body(): pl.pallas_call(functools.partial(kernel, n), out_shape=[out] * 3, in_spec...]
    ppermute x4 -> x0, waiting for transfers between devices: 42.1 us -> none  [the longest x2 18.9 us: passed_along(): return lax.ppermute(block, axis, route)]
    ppermute x4 -> x0, starting transfers between devices: 22.1 us -> none  [the longest x1 10.1 us: with_halo(): lax.ppermute(lax.slice_in_dim(block, 0, width, axis=dim), axis, backward)]
    dynamic_update_slice x8 -> x0, other arithmetic: 7.71 us -> none  [body(): lax.scan(one_head, None, (query_t, grad_t, widened[0], widened[1]))]
    reshape x9 -> x0, local copies, waits for them, and re-layouts: 7.19 us -> none  [the longest x8 7.08 us: body(): jnp.repeat(jnp.repeat(slot_mask, patch_rows, axis=0), patch_rows, axis=1)]
    unnamed x11 -> x7, local copies, waits for them, and re-layouts: 10.7 us -> 3.95 us
    another operation x3 -> x0, other arithmetic: 5.47 us -> none
  transfers between devices with their start and end apart: 4 -> 0, of which waited for: 4 -> 0; matrix products, arithmetic and copies ran while one was open for 4% -> 0% of each run, Pallas kernels for 0% -> 0%
where the time goes in v1:
time: 66.4 us; the launch traced here: 66.3 us
  Pallas kernels  61.6 us (93%)
  local copies, waits for them, and re-layouts  3.95 us (6%)
    pallas_call x1, Pallas kernels, body(): pl.pallas_call(functools.partial(kernel, n), out_shape=[out] * 3, in_spec...  61.6 us
    unnamed x7, local copies, waits for them, and re-layouts  3.95 us

profile of v1, /device:TPU:24, one launch (start us, length us, event | category | flops | bytes accessed | tf_op | source)
XLA Modules:
  0.0 66.3 jit_solution(14147131881481835430)
XLA Ops:
  0.6 61.6 %shard_map.85 = (bf16[512,512]{1,0:T(8,128)(2,1)}, bf16[512,512]{1,0:T(8,128)(2,1)}, bf16[512,512]{1,0:T(8,128)(2,1)}) custom-call(bf16[512,512]{1,0:T(8,128)(2,1)} %query.1, bf16[512,512]{1,0:T(8,128)(2,1)} %key.1, bf16[512,512]{1,0:T(8,128)(2,1)} %value.1, bf16[512,512]{1,0:T(8,128)(2,1)} %gout.1, s32[8,16]{1,0:T(8,128)} %neighbours.1, s32[1024]{0:T(1024)} %owner.1), custom_call_target="tpu_custom_call" | custom-call | tf_op jit(solution)/shard_map/pallas_call | solution.py:402
  62.3 0.0 copy-start.1
  62.3 1.9 %copy.12 = bf16[512,512]{1,0:T(8,128)(2,1)} copy(bf16[512,512]{1,0:T(8,128)(2,1)} %get-tuple-element.6) | data formatting | bytes 1048576
  64.2 0.0 copy-done.1
  64.2 0.0 copy-start
  64.2 0.8 %copy.13 = bf16[512,512]{1,0:T(8,128)(2,1)} copy(bf16[512,512]{1,0:T(8,128)(2,1)S(1)} %copy-done.1) | data formatting | bytes 1048576
  65.0 0.4 copy-done
  65.5 0.8 %copy.14 = bf16[512,512]{1,0:T(8,128)(2,1)} copy(bf16[512,512]{1,0:T(8,128)(2,1)S(1)} %copy-done) | data formatting | bytes 1048576
Async XLA Ops:
  62.3 1.9 %copy-start.1 = (bf16[512,512]{1,0:T(8,128)(2,1)S(1)}, bf16[512,512]{1,0:T(8,128)(2,1)}, u32[]{:S(2)}) copy-start(bf16[512,512]{1,0:T(8,128)(2,1)} %get-tuple-element.7) | copy-start | bytes 1572868
  64.2 1.2 %copy-start = (bf16[512,512]{1,0:T(8,128)(2,1)S(1)}, bf16[512,512]{1,0:T(8,128)(2,1)}, u32[]{:S(2)}) copy-start(bf16[512,512]{1,0:T(8,128)(2,1)} %get-tuple-element.8) | copy-start | bytes 1572868

commit v2 on v1

v2 whole, which is shorter than its diff:
```python
import functools
import math

import jax
import jax.numpy as jnp
from jax import lax
from jax.experimental import pallas as pl
from jax.experimental.pallas import tpu as pltpu
from jax.sharding import PartitionSpec as P

HEADS = 8
MESH = pl.DeviceIdType.MESH
BF16, F32 = jnp.bfloat16, jnp.float32
MASKED = -1e30
ROWS = 512
TILE = 256
PAIRS = 4
CHUNKS = PAIRS * ROWS // TILE
RING = 4
LAG_C, LAG_D = 3, 6
AHEAD = 3


def dot(left, right):
    return lax.dot_general(left, right, (((1,), (0,)), ((), ())), preferred_element_type=F32)


def dot_last(left, right):
    return lax.dot_general(left, right, (((1,), (1,)), ((), ())), preferred_element_type=F32)


def kernel(
    n,
    query, key, value, gout, neighbours, owner,
    grad_query, grad_key, grad_value,
    own_ids, near_ids, k_pair, v_pair, k_turned, q_all, g_all, bias, hot, mask_out, mask_in,
    e_own, d_own, e_near, d_near, peaks, stat_out, stat_in, stat_far,
    weights, dscores, dq_own, dq_out, dq_in,
    load_sem, bulk_send, bulk_recv, mask_send, mask_recv, stat_send, stat_recv,
    far_send, far_recv, dq_send, dq_recv,
):
    me = lax.axis_index("patch")
    target = (jnp.minimum(me + 1, n - 1), jnp.maximum(me - 1, 0))
    sends = (me < n - 1, me > 0)
    receives = (me > 0, me < n - 1)
    far_target = (jnp.minimum(me + 2, n - 1), jnp.maximum(me - 2, 0))
    far_sends = (me < n - 2, me > 1)
    far_receives = (me > 1, me < n - 2)
    scaling = 1.0 / math.sqrt(64)
    base2 = scaling * math.log2(math.e)

    barrier = pltpu.get_barrier_semaphore()
    peers = jnp.int32(0)
    for exists, peer in zip(sends + far_sends, target + far_target):
        peers = peers + exists.astype(jnp.int32)

        @pl.when(exists)
        def _(peer=peer):
            pl.semaphore_signal(barrier, inc=1, device_id={"patch": peer}, device_id_type=MESH)

    own_copy = pltpu.make_async_copy(owner, own_ids, load_sem.at[4 * PAIRS])
    near_copy = pltpu.make_async_copy(neighbours, near_ids, load_sem.at[4 * PAIRS + 1])
    own_copy.start()
    near_copy.start()

    def load(pair, array):
        lanes = pl.ds(128 * pair, 128)
        middle = pl.ds(ROWS, ROWS)
        source = (key, value, query, gout)[array].at[:, lanes]
        place = (
            k_pair.at[pair],
            v_pair.at[pair],
            q_all.at[pair, middle],
            g_all.at[pair, middle],
        )[array]
        return pltpu.make_async_copy(source, place, load_sem.at[4 * pair + array])

    for pair in range(PAIRS):
        for array in range(4):
            load(pair, array).start()

    pl.semaphore_wait(barrier, peers)

    def remote(source, place, send_sem, recv_sem, flow):
        return pltpu.make_async_remote_copy(
            src_ref=source,
            dst_ref=place,
            send_sem=send_sem,
            recv_sem=recv_sem,
            device_id={"patch": target[flow]},
            device_id_type=MESH,
        )

    def mask_copy(flow):
        return remote(
            mask_out.at[flow], mask_in.at[flow], mask_send.at[flow], mask_recv.at[flow], flow
        )

    def split(chunk):
        pair = lax.div(chunk, 2)
        first = pl.multiple_of(lax.rem(chunk, 2) * TILE, TILE)
        return pair, first

    def bulk_copy(chunk, flow, array):
        pair, first = split(chunk)
        lanes = pl.ds(pl.multiple_of(pair * 128, 128), 128)
        source = (query, gout)[array].at[pl.ds(first, TILE), lanes]
        place = (q_all, g_all)[array].at[pair, pl.ds(2 * ROWS * flow + first, TILE)]
        at = (flow, chunk, array)
        return remote(source, place, bulk_send.at[at], bulk_recv.at[at], flow)

    def stat_copy(chunk, flow):
        at = (flow, chunk)
        return remote(stat_out.at[at], stat_in.at[at], stat_send.at[at], stat_recv.at[at], flow)

    def far_copy(chunk, flow):
        at = (flow, chunk)
        return pltpu.make_async_remote_copy(
            src_ref=stat_out.at[flow, chunk, 1],
            dst_ref=stat_far.at[at],
            send_sem=far_send.at[at],
            recv_sem=far_recv.at[at],
            device_id={"patch": far_target[flow]},
            device_id_type=MESH,
        )

    def dq_copy(chunk, flow):
        at = (flow, chunk)
        return remote(dq_out.at[at], dq_in.at[at], dq_send.at[at], dq_recv.at[at], flow)

    def start(copies, when=sends):
        for flow in (0, 1):

            @pl.when(when[flow])
            def _(flow=flow):
                for copy in copies(flow):
                    copy.start()

    def wait_send(copies, when=sends):
        for flow in (0, 1):

            @pl.when(when[flow])
            def _(flow=flow):
                for copy in copies(flow):
                    copy.wait_send()

    def wait_recv(copies, when=receives):
        for flow in (0, 1):

            @pl.when(when[flow])
            def _(flow=flow):
                for copy in copies(flow):
                    copy.wait_recv()

    def bulk_copies(chunk):
        return lambda flow: [bulk_copy(chunk, flow, array) for array in (0, 1)]

    start(bulk_copies(jnp.int32(0)))

    own_copy.wait()
    near_copy.wait()
    lane = lax.broadcasted_iota(jnp.int32, (8, 128), 1)
    low_lane = lax.rem(lane, 64)
    first_id = 8 * (me - 1)
    held = [jnp.full((8, 128), -1, jnp.int32) for _ in range(3)]
    for t in range(24):
        number = first_id + t
        valid = (number >= 0) & (number < 8 * n)
        slot = own_ids[jnp.clip(number, 0, 8 * n - 1)] - first_id
        slot = jnp.where(valid, slot, -1000)
        held = [jnp.where(low_lane == slot - 8 * w, number, held[w]) for w in range(3)]
    near = near_ids[...]
    found = [jnp.zeros((8, 128), jnp.bool_) for _ in range(3)]
    for j in range(16):
        column = jnp.broadcast_to(near[:, j : j + 1], (8, 128))
        found = [found[w] | (column == held[w]) for w in range(3)]
    masks = [jnp.where(found[w] | (low_lane >= 8), 0.0, MASKED) for w in range(3)]
    mask_out[0] = masks[2]
    mask_out[1] = masks[0]
    start(lambda flow: [mask_copy(flow)])
    for chunk in range(1, AHEAD):
        start(bulk_copies(jnp.int32(chunk)))

    def spread(block, mask):
        for a in range(8):
            rows = pl.ds(ROWS * block + 64 * a, 64)
            bias[rows, :] = jnp.broadcast_to(mask[a : a + 1, :], (64, 128)).astype(BF16)

    spread(1, masks[1])
    row_slot = lax.broadcasted_iota(jnp.int32, (ROWS, 128), 0) // 64
    lane_slot = lax.rem(lax.broadcasted_iota(jnp.int32, (ROWS, 128), 1), 64)
    hot[...] = jnp.where(row_slot == lane_slot, 1.0, 0.0).astype(BF16)

    for flow in (0, 1):

        @pl.when(jnp.logical_not(receives[flow]))
        def _(flow=flow):
            rows = pl.ds(2 * ROWS * flow, ROWS)
            for pair in range(PAIRS):
                q_all[pair, rows, :] = jnp.zeros((ROWS, 128), BF16)
                g_all[pair, rows, :] = jnp.zeros((ROWS, 128), BF16)
            mask_in[flow] = jnp.full((8, 128), MASKED, F32)
            stat_in[flow] = jnp.full((CHUNKS, 2, 8, 128), MASKED, F32)
            dq_in[flow] = jnp.zeros((CHUNKS, 128, TILE), BF16)

        @pl.when(jnp.logical_not(far_receives[flow]))
        def _(flow=flow):
            stat_far[flow] = jnp.full((CHUNKS, 8, 128), MASKED, F32)

    for pair in range(PAIRS):
        for array in range(4):
            load(pair, array).wait()
    for pair in range(PAIRS):
        k_turned[pair] = k_pair[pair].T

    half = lax.broadcasted_iota(jnp.int32, (1, 128), 1) < 64
    halves = (half, jnp.logical_not(half))

    def keys_of(pair, h):
        return (
            jnp.where(halves[h], k_pair[pair], hot[...]),
            jnp.where(halves[h], v_pair[pair], jnp.zeros((), BF16)),
        )

    def scores_of(keys, values, pair, rows, h, e_ref, d_ref):
        queries = jnp.where(halves[h], q_all[pair, rows, :], bias[rows, :])
        scores = dot_last(keys, queries)
        peak = jnp.max(scores, axis=0, keepdims=True)
        raised = jnp.exp2((scores - peak) * base2)
        e_ref[...] = raised
        dweights = dot_last(values, g_all[pair, rows, :])
        d_ref[...] = dweights
        total = jnp.sum(raised, axis=0, keepdims=True)
        weighted = jnp.sum(raised * dweights, axis=0, keepdims=True)
        raised_by = peak * base2
        return raised_by, raised_by + jnp.log2(total), weighted / total

    def packed(found):
        rows = [row for peak, log_total, delta in found for row in halved(log_total)]
        rows += [row for peak, log_total, delta in found for row in halved(delta)]
        return jnp.concatenate(rows, axis=0)

    def halved(row):
        return [row[:, :128], row[:, 128:]]

    def keep_peaks(block, chunk, found):
        for h in (0, 1):
            peaks[block, chunk, h : h + 1, :] = found[h][0]

    def own_scores(pair, carry):
        both = [keys_of(pair, h) for h in (0, 1)]
        for t in (0, 1):
            chunk = 2 * pair + t
            found = []
            for h in (0, 1):
                rows = pl.ds(ROWS + TILE * t, TILE)
                found += [
                    scores_of(*both[h], pair, rows, h, e_own.at[chunk, h], d_own.at[chunk, h])
                ]
            keep_peaks(1, chunk, found)
            stat_out[0, chunk, 0] = packed(found)
            stat_out[1, chunk, 0] = packed(found)
        return carry

    lax.fori_loop(0, PAIRS, own_scores, 0)

    wait_recv(lambda flow: [mask_copy(flow)])
    spread(0, mask_in[0])
    spread(2, mask_in[1])

    def near_scores(chunk):
        pair, first = split(chunk)
        slot = lax.rem(chunk, RING)
        found = [[], []]
        for h in (0, 1):
            keys, values = keys_of(pair, h)
            for side in (0, 1):
                rows = pl.ds(2 * ROWS * side + first, TILE)
                e_ref, d_ref = e_near.at[slot, side, h], d_near.at[slot, side, h]
                found[side] += [scores_of(keys, values, pair, rows, h, e_ref, d_ref)]
        for side in (0, 1):
            keep_peaks(2 * side, chunk, found[side])
            stat_out[1 - side, chunk, 1] = packed(found[side])

    def combined(parts):
        logs, deltas = [part[:4] for part in parts], [part[4:] for part in parts]
        top = functools.reduce(jnp.maximum, logs)
        scales = [jnp.exp2(one - top) for one in logs]
        total = sum(scales)
        delta = sum(scale * one for scale, one in zip(scales, deltas)) / total
        return top + jnp.log2(total), delta

    def finish(chunk):
        pair, first = split(chunk)
        slot = lax.rem(chunk, RING)
        finals = [
            combined([stat_out[1, chunk, 1], stat_in[0, chunk, 0], stat_far[0, chunk]]),
            combined([stat_out[0, chunk, 0], stat_in[0, chunk, 1], stat_in[1, chunk, 1]]),
            combined([stat_out[0, chunk, 1], stat_in[1, chunk, 0], stat_far[1, chunk]]),
        ]
        for h in (0, 1):
            turned = k_turned[pair, pl.ds(64 * h, 64), :]
            for block in range(3):
                side = block // 2
                if block == 1:
                    e_ref, d_ref = e_own.at[chunk, h], d_own.at[chunk, h]
                else:
                    e_ref, d_ref = e_near.at[slot, side, h], d_near.at[slot, side, h]
                log_total, delta = (
                    jnp.concatenate([one[2 * h : 2 * h + 1], one[2 * h + 1 : 2 * h + 2]], axis=1)
                    for one in finals[block]
                )
                weight = e_ref[...] * jnp.exp2(peaks[block, chunk, h : h + 1, :] - log_total)
                dscore = (weight * (d_ref[...] - delta)).astype(BF16)
                lanes = pl.ds(ROWS * block + first, TILE)
                weights[h, :, lanes] = weight.astype(BF16)
                dscores[h, :, lanes] = dscore
                part = dot(turned, dscore)
                if block == 1:
                    dq_own[chunk, pl.ds(64 * h, 64), :] = part
                else:
                    dq_out[1 - side, chunk, pl.ds(64 * h, 64), :] = part.astype(BF16)

    def key_gradients(pair):
        dv = [dot(weights[h], g_all[pair]) for h in (0, 1)]
        dk = [dot(dscores[h], q_all[pair]) for h in (0, 1)]
        grad_value[pair] = jnp.where(half, dv[0], dv[1]).astype(BF16)
        grad_key[pair] = (jnp.where(half, dk[0], dk[1]) * scaling).astype(BF16)

    def query_gradients(chunk):
        total = dq_own[chunk] + dq_in[0, chunk].astype(F32) + dq_in[1, chunk].astype(F32)
        grad_query[chunk] = (total * scaling).T.astype(BF16)

    def step(s, carry):
        @pl.when(s < CHUNKS)
        def _():
            wait_recv(bulk_copies(s))
            near_scores(s)
            start(lambda flow: [stat_copy(s, flow)])
            start(lambda flow: [far_copy(s, flow)], far_sends)

            @pl.when(s + AHEAD < CHUNKS)
            def _():
                start(bulk_copies(s + AHEAD))

        @pl.when((s >= LAG_C) & (s < CHUNKS + LAG_C))
        def _():
            chunk = s - LAG_C
            wait_recv(lambda flow: [stat_copy(chunk, flow)])
            wait_recv(lambda flow: [far_copy(chunk, flow)], far_receives)
            finish(chunk)

            @pl.when(chunk == 1)
            def _():
                start(lambda flow: [dq_copy(0, flow)])

            @pl.when(chunk >= 1)
            def _():
                start(lambda flow: [dq_copy(chunk, flow)])

            @pl.when(lax.rem(chunk, 2) == 1)
            def _():
                key_gradients(lax.div(chunk, 2))

        @pl.when(s >= LAG_D)
        def _():
            chunk = s - LAG_D
            wait_recv(lambda flow: [dq_copy(chunk, flow)])
            query_gradients(chunk)

        return carry

    lax.fori_loop(0, CHUNKS + LAG_D, step, 0)

    wait_send(lambda flow: [mask_copy(flow)])

    def drain(chunk, carry):
        wait_send(
            lambda flow: [
                *bulk_copies(chunk)(flow),
                stat_copy(chunk, flow),
                dq_copy(chunk, flow),
            ]
        )
        wait_send(lambda flow: [far_copy(chunk, flow)], far_sends)
        return carry

    lax.fori_loop(0, CHUNKS, drain, 0)


def write_out(dq, dk, dv, grad_query, grad_key, grad_value, sem):
    copies = []
    for chunk in range(CHUNKS):
        place = (pl.ds(TILE * (chunk % 2), TILE), pl.ds(128 * (chunk // 2), 128))
        copies.append((dq.at[chunk], grad_query.at[place]))
    for pair in range(PAIRS):
        place = (slice(None), pl.ds(128 * pair, 128))
        copies.append((dk.at[pair], grad_key.at[place]))
        copies.append((dv.at[pair], grad_value.at[place]))
    copies = [pltpu.make_async_copy(*one, sem.at[i]) for i, one in enumerate(copies)]
    for copy in copies:
        copy.start()
    for copy in copies:
        copy.wait()


def body(n, query_rows, key_rows, value_rows, grad_output, neighbours, owner):
    rows, features = query_rows.shape
    out = jax.ShapeDtypeStruct((rows, features), BF16)
    far, near = pl.BlockSpec(memory_space=pl.ANY), pl.BlockSpec(memory_space=pltpu.VMEM)
    dma = pltpu.SemaphoreType.DMA
    wide = ROWS * 3
    parts = pl.pallas_call(
        functools.partial(kernel, n),
        out_shape=[
            jax.ShapeDtypeStruct((CHUNKS, TILE, 128), BF16),
            jax.ShapeDtypeStruct((PAIRS, ROWS, 128), BF16),
            jax.ShapeDtypeStruct((PAIRS, ROWS, 128), BF16),
        ],
        in_specs=[far] * 6,
        out_specs=[near] * 3,
        scratch_shapes=[
            pltpu.SMEM(owner.shape, jnp.int32),
            pltpu.VMEM(neighbours.shape, jnp.int32),
            pltpu.VMEM((PAIRS, ROWS, 128), BF16),
            pltpu.VMEM((PAIRS, ROWS, 128), BF16),
            pltpu.VMEM((PAIRS, 128, ROWS), BF16),
            pltpu.VMEM((PAIRS, wide, 128), BF16),
            pltpu.VMEM((PAIRS, wide, 128), BF16),
            pltpu.VMEM((wide, 128), BF16),
            pltpu.VMEM((ROWS, 128), BF16),
            pltpu.VMEM((2, 8, 128), F32),
            pltpu.VMEM((2, 8, 128), F32),
            pltpu.VMEM((CHUNKS, 2, ROWS, TILE), F32),
            pltpu.VMEM((CHUNKS, 2, ROWS, TILE), F32),
            pltpu.VMEM((RING, 2, 2, ROWS, TILE), F32),
            pltpu.VMEM((RING, 2, 2, ROWS, TILE), F32),
            pltpu.VMEM((3, CHUNKS, 8, TILE), F32),
            pltpu.VMEM((2, CHUNKS, 2, 8, 128), F32),
            pltpu.VMEM((2, CHUNKS, 2, 8, 128), F32),
            pltpu.VMEM((2, CHUNKS, 8, 128), F32),
            pltpu.VMEM((2, ROWS, wide), BF16),
            pltpu.VMEM((2, ROWS, wide), BF16),
            pltpu.VMEM((CHUNKS, 128, TILE), F32),
            pltpu.VMEM((2, CHUNKS, 128, TILE), BF16),
            pltpu.VMEM((2, CHUNKS, 128, TILE), BF16),
            dma((4 * PAIRS + 2,)),
            dma((2, CHUNKS, 2)),
            dma((2, CHUNKS, 2)),
            dma((2,)),
            dma((2,)),
            dma((2, CHUNKS)),
            dma((2, CHUNKS)),
            dma((2, CHUNKS)),
            dma((2, CHUNKS)),
            dma((2, CHUNKS)),
            dma((2, CHUNKS)),
        ],
        compiler_params=pltpu.CompilerParams(
            collective_id=0, has_side_effects=True, vmem_limit_bytes=56 << 20
        ),
    )(query_rows, key_rows, value_rows, grad_output, neighbours, owner)
    return pl.pallas_call(
        write_out,
        out_shape=[out] * 3,
        in_specs=[near] * 3,
        out_specs=[far] * 3,
        scratch_shapes=[dma((CHUNKS + 2 * PAIRS,))],
    )(*parts)


def solution(mesh):
    split = P(("scene", "patch"), None)
    return jax.shard_map(
        functools.partial(body, mesh.shape["patch"]),
        mesh=mesh,
        in_specs=(split, split, split, split, split, P("scene")),
        out_specs=(split, split, split),
        check_vma=False,
    )
```

time: 66.4 us -> 58.4 us (0.88)
  Pallas kernels: 61.6 us -> 57.6 us
  local copies, waits for them, and re-layouts: 3.95 us -> 0 us
    pallas_call x1 -> x2, Pallas kernels: 61.6 us -> 57.6 us  [the longest x1 55 us: body(): pl.pallas_call(functools.partial(kernel, n), out_shape=[jax.ShapeDtypeStr...]
    unnamed x7 -> x0, local copies, waits for them, and re-layouts: 3.95 us -> none
where the time goes in v2:
time: 58.4 us; the launch traced here: 58.2 us
  Pallas kernels  57.6 us (99%)
  between operations  0.64 us (1%)
    pallas_call x1, Pallas kernels, body(): pl.pallas_call(functools.partial(kernel, n), out_shape=[jax.ShapeDtypeStr...  55 us
    pallas_call x1, Pallas kernels, body(): pl.pallas_call(write_out, out_shape=[out] * 3, in_specs=[near] * 3, out_s...  2.62 us

profile of v2, /device:TPU:24, one launch (start us, length us, event | category | flops | bytes accessed | tf_op | source)
XLA Modules:
  0.0 58.2 jit_solution(16918620995785215004)
XLA Ops:
  0.6 55.0 %shard_map.85 = (bf16[8,256,128]{2,1,0:T(8,128)(2,1)}, bf16[4,512,128]{2,1,0:T(8,128)(2,1)}, bf16[4,512,128]{2,1,0:T(8,128)(2,1)}) custom-call(bf16[512,512]{1,0:T(8,128)(2,1)} %query.1, bf16[512,512]{1,0:T(8,128)(2,1)} %key.1, bf16[512,512]{1,0:T(8,128)(2,1)} %value.1, bf16[512,512]{1,0:T(8,128)(2,1)} %gout.1, s32[8,16]{1,0:T(8,128)} %neighbours.1, s32[1024]{0:T(1024)} %owner.1), custom_call_target="tpu_custom_call" | custom-call | tf_op jit(solution)/shard_map/pallas_call | solution.py:413
  55.6 2.6 %shard_map.86 = (bf16[512,512]{1,0:T(8,128)(2,1)}, bf16[512,512]{1,0:T(8,128)(2,1)}, bf16[512,512]{1,0:T(8,128)(2,1)}) custom-call(bf16[8,256,128]{2,1,0:T(8,128)(2,1)} %get-tuple-element.6.dq, bf16[4,512,128]{2,1,0:T(8,128)(2,1)} %get-tuple-element.7.dk, bf16[4,512,128]{2,1,0:T(8,128)(2,1)} %get-tuple-element.8.dv), custom_call_target="tpu_custom_call" | custom-call | tf_op jit(solution)/shard_map/pallas_call | solution.py:463

commit v3 on v2

--- a/solution.py
+++ b/solution.py
@@ -17,7 +17,7 @@
 PAIRS = 4
 CHUNKS = PAIRS * ROWS // TILE
 RING = 4
-LAG_C, LAG_D = 3, 6
+LAG_C, LAG_D = 3, 7
 AHEAD = 3
 
 
@@ -75,10 +75,6 @@
         )[array]
         return pltpu.make_async_copy(source, place, load_sem.at[4 * pair + array])
 
-    for pair in range(PAIRS):
-        for array in range(4):
-            load(pair, array).start()
-
     pl.semaphore_wait(barrier, peers)
 
     def remote(source, place, send_sem, recv_sem, flow):
@@ -124,8 +120,8 @@
             device_id_type=MESH,
         )
 
-    def dq_copy(chunk, flow):
-        at = (flow, chunk)
+    def dq_copy(chunk, flow, h):
+        at = (flow, chunk, h)
         return remote(dq_out.at[at], dq_in.at[at], dq_send.at[at], dq_recv.at[at], flow)
 
     def start(copies, when=sends):
@@ -156,6 +152,10 @@
         return lambda flow: [bulk_copy(chunk, flow, array) for array in (0, 1)]
 
     start(bulk_copies(jnp.int32(0)))
+
+    for pair in range(PAIRS):
+        for array in range(4):
+            load(pair, array).start()
 
     own_copy.wait()
     near_copy.wait()
@@ -201,7 +201,7 @@
                 g_all[pair, rows, :] = jnp.zeros((ROWS, 128), BF16)
             mask_in[flow] = jnp.full((8, 128), MASKED, F32)
             stat_in[flow] = jnp.full((CHUNKS, 2, 8, 128), MASKED, F32)
-            dq_in[flow] = jnp.zeros((CHUNKS, 128, TILE), BF16)
+            dq_in[flow] = jnp.zeros((CHUNKS, 2, 64, TILE), BF16)
 
         @pl.when(jnp.logical_not(far_receives[flow]))
         def _(flow=flow):
@@ -298,28 +298,42 @@
             combined([stat_out[0, chunk, 0], stat_in[0, chunk, 1], stat_in[1, chunk, 1]]),
             combined([stat_out[0, chunk, 1], stat_in[1, chunk, 0], stat_far[1, chunk]]),
         ]
+
+        def one(h, block):
+            side = block // 2
+            if block == 1:
+                e_ref, d_ref = e_own.at[chunk, h], d_own.at[chunk, h]
+            else:
+                e_ref, d_ref = e_near.at[slot, side, h], d_near.at[slot, side, h]
+            log_total, delta = (
+                jnp.concatenate([one[2 * h : 2 * h + 1], one[2 * h + 1 : 2 * h + 2]], axis=1)
+                for one in finals[block]
+            )
+            weight = e_ref[...] * jnp.exp2(peaks[block, chunk, h : h + 1, :] - log_total)
+            dscore = (weight * (d_ref[...] - delta)).astype(BF16)
+            lanes = pl.ds(ROWS * block + first, TILE)
+            weights[h, :, lanes] = weight.astype(BF16)
+            dscores[h, :, lanes] = dscore
+            part = dot(k_turned[pair, pl.ds(64 * h, 64), :], dscore)
+            if block == 1:
+                dq_own[chunk, pl.ds(64 * h, 64), :] = part
+            else:
+                dq_out[1 - side, chunk, h] = part.astype(BF16)
+
         for h in (0, 1):
-            turned = k_turned[pair, pl.ds(64 * h, 64), :]
-            for block in range(3):
-                side = block // 2
-                if block == 1:
-                    e_ref, d_ref = e_own.at[chunk, h], d_own.at[chunk, h]
-                else:
-                    e_ref, d_ref = e_near.at[slot, side, h], d_near.at[slot, side, h]
-                log_total, delta = (
-                    jnp.concatenate([one[2 * h : 2 * h + 1], one[2 * h + 1 : 2 * h + 2]], axis=1)
-                    for one in finals[block]
-                )
-                weight = e_ref[...] * jnp.exp2(peaks[block, chunk, h : h + 1, :] - log_total)
-                dscore = (weight * (d_ref[...] - delta)).astype(BF16)
-                lanes = pl.ds(ROWS * block + first, TILE)
-                weights[h, :, lanes] = weight.astype(BF16)
-                dscores[h, :, lanes] = dscore
-                part = dot(turned, dscore)
-                if block == 1:
-                    dq_own[chunk, pl.ds(64 * h, 64), :] = part
-                else:
-                    dq_out[1 - side, chunk, pl.ds(64 * h, 64), :] = part.astype(BF16)
+            one(h, 0)
+            one(h, 2)
+
+            @pl.when(chunk >= 1)
+            def _(h=h):
+                start(lambda flow: [dq_copy(chunk, flow, h)])
+
+        @pl.when(chunk == 1)
+        def _():
+            start(lambda flow: [dq_copy(0, flow, h) for h in (0, 1)])
+
+        for h in (0, 1):
+            one(h, 1)
 
     def key_gradients(pair):
         dv = [dot(weights[h], g_all[pair]) for h in (0, 1)]
@@ -328,7 +342,8 @@
         grad_key[pair] = (jnp.where(half, dk[0], dk[1]) * scaling).astype(BF16)
 
     def query_gradients(chunk):
-        total = dq_own[chunk] + dq_in[0, chunk].astype(F32) + dq_in[1, chunk].astype(F32)
+        near = [dq_in[flow, chunk].reshape(128, TILE).astype(F32) for flow in (0, 1)]
+        total = dq_own[chunk] + near[0] + near[1]
         grad_query[chunk] = (total * scaling).T.astype(BF16)
 
     def step(s, carry):
@@ -350,27 +365,21 @@
             wait_recv(lambda flow: [far_copy(chunk, flow)], far_receives)
             finish(chunk)
 
-            @pl.when(chunk == 1)
-            def _():
-                start(lambda flow: [dq_copy(0, flow)])
-
-            @pl.when(chunk >= 1)
-            def _():
-                start(lambda flow: [dq_copy(chunk, flow)])
-
             @pl.when(lax.rem(chunk, 2) == 1)
             def _():
                 key_gradients(lax.div(chunk, 2))
 
         @pl.when(s >= LAG_D)
         def _():
-            chunk = s - LAG_D
-            wait_recv(lambda flow: [dq_copy(chunk, flow)])
-            query_gradients(chunk)
+            sum_queries(s - LAG_D)
 
         return carry
 
-    lax.fori_loop(0, CHUNKS + LAG_D, step, 0)
+    def sum_queries(chunk):
+        wait_recv(lambda flow: [dq_copy(chunk, flow, h) for h in (0, 1)])
+        query_gradients(chunk)
+
+    lax.fori_loop(0, CHUNKS + LAG_D - 1, step, 0)
 
     wait_send(lambda flow: [mask_copy(flow)])
 
@@ -379,13 +388,15 @@
             lambda flow: [
                 *bulk_copies(chunk)(flow),
                 stat_copy(chunk, flow),
-                dq_copy(chunk, flow),
+                dq_copy(chunk, flow, 0),
+                dq_copy(chunk, flow, 1),
             ]
         )
         wait_send(lambda flow: [far_copy(chunk, flow)], far_sends)
         return carry
 
     lax.fori_loop(0, CHUNKS, drain, 0)
+    sum_queries(CHUNKS - 1)
 
 
 def write_out(dq, dk, dv, grad_query, grad_key, grad_value, sem):
@@ -413,9 +424,9 @@
     parts = pl.pallas_call(
         functools.partial(kernel, n),
         out_shape=[
-            jax.ShapeDtypeStruct((CHUNKS, TILE, 128), BF16),
-            jax.ShapeDtypeStruct((PAIRS, ROWS, 128), BF16),
-            jax.ShapeDtypeStruct((PAIRS, ROWS, 128), BF16),
+            pltpu.VMEM((CHUNKS, TILE, 128), BF16),
+            pltpu.VMEM((PAIRS, ROWS, 128), BF16),
+            pltpu.VMEM((PAIRS, ROWS, 128), BF16),
         ],
         in_specs=[far] * 6,
         out_specs=[near] * 3,
@@ -442,8 +453,8 @@
             pltpu.VMEM((2, ROWS, wide), BF16),
             pltpu.VMEM((2, ROWS, wide), BF16),
             pltpu.VMEM((CHUNKS, 128, TILE), F32),
-            pltpu.VMEM((2, CHUNKS, 128, TILE), BF16),
-            pltpu.VMEM((2, CHUNKS, 128, TILE), BF16),
+            pltpu.VMEM((2, CHUNKS, 2, 64, TILE), BF16),
+            pltpu.VMEM((2, CHUNKS, 2, 64, TILE), BF16),
             dma((4 * PAIRS + 2,)),
             dma((2, CHUNKS, 2)),
             dma((2, CHUNKS, 2)),
@@ -453,11 +464,11 @@
             dma((2, CHUNKS)),
             dma((2, CHUNKS)),
             dma((2, CHUNKS)),
-            dma((2, CHUNKS)),
-            dma((2, CHUNKS)),
+            dma((2, CHUNKS, 2)),
+            dma((2, CHUNKS, 2)),
         ],
         compiler_params=pltpu.CompilerParams(
-            collective_id=0, has_side_effects=True, vmem_limit_bytes=56 << 20
+            collective_id=0, has_side_effects=True, vmem_limit_bytes=58 << 20
         ),
     )(query_rows, key_rows, value_rows, grad_output, neighbours, owner)
     return pl.pallas_call(
@@ -466,7 +477,7 @@
         in_specs=[near] * 3,
         out_specs=[far] * 3,
         scratch_shapes=[dma((CHUNKS + 2 * PAIRS,))],
-    )(*parts)
+    )(*[pltpu.with_memory_space_constraint(one, pltpu.VMEM) for one in parts])
 
 
 def solution(mesh):

time: 58.4 us -> 55.2 us (0.945)
  Pallas kernels: 57.6 us -> 54.5 us
    pallas_call x1, Pallas kernels: 55 us -> 53.2 us  [body(): pl.pallas_call(functools.partial(kernel, n), out_shape=[pltpu.VMEM((CHUNK...]
    pallas_call x1, Pallas kernels: 2.62 us -> 1.27 us  [body(): pl.pallas_call(write_out, out_shape=[out] * 3, in_specs=[near] * 3, out_s...]
where the time goes in v3:
time: 55.2 us; the launch traced here: 55.1 us
  Pallas kernels  54.5 us (99%)
  between operations  0.64 us (1%)
    pallas_call x1, Pallas kernels, body(): pl.pallas_call(functools.partial(kernel, n), out_shape=[pltpu.VMEM((CHUNK...  53.2 us
    pallas_call x1, Pallas kernels, body(): pl.pallas_call(write_out, out_shape=[out] * 3, in_specs=[near] * 3, out_s...  1.27 us

profile of v3, /device:TPU:24, one launch (start us, length us, event | category | flops | bytes accessed | tf_op | source)
XLA Modules:
  0.0 55.1 jit_solution(18225656002447266944)
XLA Ops:
  0.6 53.2 %shard_map.85 = (bf16[8,256,128]{2,1,0:T(8,128)(2,1)S(1)}, bf16[4,512,128]{2,1,0:T(8,128)(2,1)S(1)}, bf16[4,512,128]{2,1,0:T(8,128)(2,1)S(1)}) custom-call(bf16[512,512]{1,0:T(8,128)(2,1)} %query.1, bf16[512,512]{1,0:T(8,128)(2,1)} %key.1, bf16[512,512]{1,0:T(8,128)(2,1)} %value.1, bf16[512,512]{1,0:T(8,128)(2,1)} %gout.1, s32[8,16]{1,0:T(8,128)} %neighbours.1, ...), custom_call_target="tpu_custom_call" | custom-call | tf_op jit(solution)/shard_map/pallas_call | solution.py:424
  53.9 1.3 %shard_map.86 = (bf16[512,512]{1,0:T(8,128)(2,1)}, bf16[512,512]{1,0:T(8,128)(2,1)}, bf16[512,512]{1,0:T(8,128)(2,1)}) custom-call(bf16[8,256,128]{2,1,0:T(8,128)(2,1)S(1)} %get-tuple-element.6.dq, bf16[4,512,128]{2,1,0:T(8,128)(2,1)S(1)} %get-tuple-element.7.dk, bf16[4,512,128]{2,1,0:T(8,128)(2,1)S(1)} %get-tuple-element.8.dv), custom_call_target="tpu_custom_call" | custom-call | tf_op jit(solution)/shard_map/pallas_call | solution.py:474

commit v4 on v3

--- a/solution.py
+++ b/solution.py
@@ -33,11 +33,10 @@
     n,
     query, key, value, gout, neighbours, owner,
     grad_query, grad_key, grad_value,
-    own_ids, near_ids, k_pair, v_pair, k_turned, q_all, g_all, bias, hot, mask_out, mask_in,
-    e_own, d_own, e_near, d_near, peaks, stat_out, stat_in, stat_far,
+    own_ids, near_ids, k_pair, v_pair, k_turned, rows_all, bias, hot, mask_out, mask_in,
+    e_own, d_own, e_near, d_near, peaks, stat_out, stat_in,
     weights, dscores, dq_own, dq_out, dq_in,
-    load_sem, bulk_send, bulk_recv, mask_send, mask_recv, stat_send, stat_recv,
-    far_send, far_recv, dq_send, dq_recv,
+    load_sem, bulk_send, bulk_recv, mask_send, mask_recv, stat_send, stat_recv, far_send, dq_send,
 ):
     me = lax.axis_index("patch")
     target = (jnp.minimum(me + 1, n - 1), jnp.maximum(me - 1, 0))
@@ -58,8 +57,8 @@
         def _(peer=peer):
             pl.semaphore_signal(barrier, inc=1, device_id={"patch": peer}, device_id_type=MESH)
 
-    own_copy = pltpu.make_async_copy(owner, own_ids, load_sem.at[4 * PAIRS])
-    near_copy = pltpu.make_async_copy(neighbours, near_ids, load_sem.at[4 * PAIRS + 1])
+    own_copy = pltpu.make_async_copy(owner, own_ids, load_sem.at[4])
+    near_copy = pltpu.make_async_copy(neighbours, near_ids, load_sem.at[5])
     own_copy.start()
     near_copy.start()
 
@@ -70,10 +69,10 @@
         place = (
             k_pair.at[pair],
             v_pair.at[pair],
-            q_all.at[pair, middle],
-            g_all.at[pair, middle],
+            rows_all.at[pair, 0, middle],
+            rows_all.at[pair, 1, middle],
         )[array]
-        return pltpu.make_async_copy(source, place, load_sem.at[4 * pair + array])
+        return pltpu.make_async_copy(source, place, load_sem.at[array])
 
     pl.semaphore_wait(barrier, peers)
 
@@ -101,28 +100,52 @@
         pair, first = split(chunk)
         lanes = pl.ds(pl.multiple_of(pair * 128, 128), 128)
         source = (query, gout)[array].at[pl.ds(first, TILE), lanes]
-        place = (q_all, g_all)[array].at[pair, pl.ds(2 * ROWS * flow + first, TILE)]
-        at = (flow, chunk, array)
-        return remote(source, place, bulk_send.at[at], bulk_recv.at[at], flow)
+        place = rows_all.at[pair, array, pl.ds(2 * ROWS * flow + first, TILE)]
+        return remote(source, place, bulk_send.at[flow], bulk_recv.at[flow, chunk], flow)
+
+    def whole(place, send_sem, recv_sem, flow):
+        return remote(place, place, send_sem, recv_sem, flow)
+
+    def bulk_arrival(chunk, flow):
+        pair, first = split(chunk)
+        place = rows_all.at[pair, :, pl.ds(2 * ROWS * flow + first, TILE)]
+        return whole(place, bulk_send.at[flow], bulk_recv.at[flow, chunk], flow)
 
     def stat_copy(chunk, flow):
+        place = stat_in.at[flow, chunk, pl.ds(0, 2)]
         at = (flow, chunk)
-        return remote(stat_out.at[at], stat_in.at[at], stat_send.at[at], stat_recv.at[at], flow)
+        return remote(stat_out.at[at], place, stat_send.at[flow], stat_recv.at[at], flow)
 
     def far_copy(chunk, flow):
-        at = (flow, chunk)
         return pltpu.make_async_remote_copy(
             src_ref=stat_out.at[flow, chunk, 1],
-            dst_ref=stat_far.at[at],
-            send_sem=far_send.at[at],
-            recv_sem=far_recv.at[at],
+            dst_ref=stat_in.at[flow, chunk, 2],
+            send_sem=far_send.at[flow],
+            recv_sem=stat_recv.at[flow, chunk],
             device_id={"patch": far_target[flow]},
             device_id_type=MESH,
         )
 
+    def wait_stats(chunk):
+        for flow in (0, 1):
+
+            @pl.when(far_receives[flow])
+            def _(flow=flow):
+                at = (flow, chunk)
+                whole(stat_in.at[at], stat_send.at[flow], stat_recv.at[at], flow).wait_recv()
+
+            @pl.when(receives[flow] & jnp.logical_not(far_receives[flow]))
+            def _(flow=flow):
+                stat_copy(chunk, flow).wait_recv()
+
     def dq_copy(chunk, flow, h):
-        at = (flow, chunk, h)
-        return remote(dq_out.at[at], dq_in.at[at], dq_send.at[at], dq_recv.at[at], flow)
+        at = (flow, chunk)
+        source, place = (ref.at[flow, chunk, h] for ref in (dq_out, dq_in))
+        return remote(source, place, dq_send.at[flow], bulk_recv.at[at], flow)
+
+    def dq_arrival(chunk, flow):
+        at = (flow, chunk)
+        return whole(dq_in.at[at], dq_send.at[flow], bulk_recv.at[at], flow)
 
     def start(copies, when=sends):
         for flow in (0, 1):
@@ -197,19 +220,19 @@
         def _(flow=flow):
             rows = pl.ds(2 * ROWS * flow, ROWS)
             for pair in range(PAIRS):
-                q_all[pair, rows, :] = jnp.zeros((ROWS, 128), BF16)
-                g_all[pair, rows, :] = jnp.zeros((ROWS, 128), BF16)
+                rows_all[pair, :, rows, :] = jnp.zeros((2, ROWS, 128), BF16)
             mask_in[flow] = jnp.full((8, 128), MASKED, F32)
-            stat_in[flow] = jnp.full((CHUNKS, 2, 8, 128), MASKED, F32)
+            stat_in[flow, :, 0:2] = jnp.full((CHUNKS, 2, 8, 128), MASKED, F32)
             dq_in[flow] = jnp.zeros((CHUNKS, 2, 64, TILE), BF16)
 
         @pl.when(jnp.logical_not(far_receives[flow]))
         def _(flow=flow):
-            stat_far[flow] = jnp.full((CHUNKS, 8, 128), MASKED, F32)
-
-    for pair in range(PAIRS):
-        for array in range(4):
-            load(pair, array).wait()
+            stat_in[flow, :, 2] = jnp.full((CHUNKS, 8, 128), MASKED, F32)
+
+    middle = pl.ds(ROWS, ROWS)
+    places = (k_pair, v_pair, rows_all.at[:, 0, middle], rows_all.at[:, 1, middle])
+    for array, place in enumerate(places):
+        pltpu.make_async_copy(place, place, load_sem.at[array]).wait()
     for pair in range(PAIRS):
         k_turned[pair] = k_pair[pair].T
 
@@ -223,12 +246,12 @@
         )
 
     def scores_of(keys, values, pair, rows, h, e_ref, d_ref):
-        queries = jnp.where(halves[h], q_all[pair, rows, :], bias[rows, :])
+        queries = jnp.where(halves[h], rows_all[pair, 0, rows, :], bias[rows, :])
         scores = dot_last(keys, queries)
         peak = jnp.max(scores, axis=0, keepdims=True)
         raised = jnp.exp2((scores - peak) * base2)
         e_ref[...] = raised
-        dweights = dot_last(values, g_all[pair, rows, :])
+        dweights = dot_last(values, rows_all[pair, 1, rows, :])
         d_ref[...] = dweights
         total = jnp.sum(raised, axis=0, keepdims=True)
         weighted = jnp.sum(raised * dweights, axis=0, keepdims=True)
@@ -294,9 +317,9 @@
         pair, first = split(chunk)
         slot = lax.rem(chunk, RING)
         finals = [
-            combined([stat_out[1, chunk, 1], stat_in[0, chunk, 0], stat_far[0, chunk]]),
+            combined([stat_out[1, chunk, 1], stat_in[0, chunk, 0], stat_in[0, chunk, 2]]),
             combined([stat_out[0, chunk, 0], stat_in[0, chunk, 1], stat_in[1, chunk, 1]]),
-            combined([stat_out[0, chunk, 1], stat_in[1, chunk, 0], stat_far[1, chunk]]),
+            combined([stat_out[0, chunk, 1], stat_in[1, chunk, 0], stat_in[1, chunk, 2]]),
         ]
 
         def one(h, block):
@@ -312,8 +335,9 @@
             weight = e_ref[...] * jnp.exp2(peaks[block, chunk, h : h + 1, :] - log_total)
             dscore = (weight * (d_ref[...] - delta)).astype(BF16)
             lanes = pl.ds(ROWS * block + first, TILE)
-            weights[h, :, lanes] = weight.astype(BF16)
-            dscores[h, :, lanes] = dscore
+            rows = pl.ds(ROWS * h, ROWS)
+            weights[rows, lanes] = weight.astype(BF16)
+            dscores[rows, lanes] = dscore
             part = dot(k_turned[pair, pl.ds(64 * h, 64), :], dscore)
             if block == 1:
                 dq_own[chunk, pl.ds(64 * h, 64), :] = part
@@ -336,20 +360,23 @@
             one(h, 1)
 
     def key_gradients(pair):
-        dv = [dot(weights[h], g_all[pair]) for h in (0, 1)]
-        dk = [dot(dscores[h], q_all[pair]) for h in (0, 1)]
-        grad_value[pair] = jnp.where(half, dv[0], dv[1]).astype(BF16)
-        grad_key[pair] = (jnp.where(half, dk[0], dk[1]) * scaling).astype(BF16)
+        dv = dot(weights[...], rows_all[pair, 1])
+        dk = dot(dscores[...], rows_all[pair, 0])
+        lanes = pl.ds(pl.multiple_of(pair * 128, 128), 128)
+        grad_value[:, lanes] = jnp.where(half, dv[:ROWS], dv[ROWS:]).astype(BF16)
+        grad_key[:, lanes] = (jnp.where(half, dk[:ROWS], dk[ROWS:]) * scaling).astype(BF16)
 
     def query_gradients(chunk):
         near = [dq_in[flow, chunk].reshape(128, TILE).astype(F32) for flow in (0, 1)]
         total = dq_own[chunk] + near[0] + near[1]
-        grad_query[chunk] = (total * scaling).T.astype(BF16)
+        pair, first = split(chunk)
+        lanes = pl.ds(pl.multiple_of(pair * 128, 128), 128)
+        grad_query[pl.ds(first, TILE), lanes] = (total * scaling).T.astype(BF16)
 
     def step(s, carry):
         @pl.when(s < CHUNKS)
         def _():
-            wait_recv(bulk_copies(s))
+            wait_recv(lambda flow: [bulk_arrival(s, flow)])
             near_scores(s)
             start(lambda flow: [stat_copy(s, flow)])
             start(lambda flow: [far_copy(s, flow)], far_sends)
@@ -361,8 +388,7 @@
         @pl.when((s >= LAG_C) & (s < CHUNKS + LAG_C))
         def _():
             chunk = s - LAG_C
-            wait_recv(lambda flow: [stat_copy(chunk, flow)])
-            wait_recv(lambda flow: [far_copy(chunk, flow)], far_receives)
+            wait_stats(chunk)
             finish(chunk)
 
             @pl.when(lax.rem(chunk, 2) == 1)
@@ -376,39 +402,34 @@
         return carry
 
     def sum_queries(chunk):
-        wait_recv(lambda flow: [dq_copy(chunk, flow, h) for h in (0, 1)])
+        wait_recv(lambda flow: [dq_arrival(chunk, flow)])
         query_gradients(chunk)
 
     lax.fori_loop(0, CHUNKS + LAG_D - 1, step, 0)
 
-    wait_send(lambda flow: [mask_copy(flow)])
-
-    def drain(chunk, carry):
-        wait_send(
-            lambda flow: [
-                *bulk_copies(chunk)(flow),
-                stat_copy(chunk, flow),
-                dq_copy(chunk, flow, 0),
-                dq_copy(chunk, flow, 1),
-            ]
-        )
-        wait_send(lambda flow: [far_copy(chunk, flow)], far_sends)
-        return carry
-
-    lax.fori_loop(0, CHUNKS, drain, 0)
+    wait_send(
+        lambda flow: [
+            mask_copy(flow),
+            whole(rows_all.at[:, :, middle], bulk_send.at[flow], bulk_recv.at[flow, 0], flow),
+            whole(stat_out.at[flow], stat_send.at[flow], stat_recv.at[flow, 0], flow),
+            whole(dq_out.at[flow], dq_send.at[flow], bulk_recv.at[flow, 0], flow),
+        ]
+    )
+    wait_send(
+        lambda flow: [
+            whole(stat_out.at[flow, :, 1], far_send.at[flow], stat_recv.at[flow, 0], flow)
+        ],
+        far_sends,
+    )
     sum_queries(CHUNKS - 1)
 
 
-def write_out(dq, dk, dv, grad_query, grad_key, grad_value, sem):
-    copies = []
-    for chunk in range(CHUNKS):
-        place = (pl.ds(TILE * (chunk % 2), TILE), pl.ds(128 * (chunk // 2), 128))
-        copies.append((dq.at[chunk], grad_query.at[place]))
-    for pair in range(PAIRS):
-        place = (slice(None), pl.ds(128 * pair, 128))
-        copies.append((dk.at[pair], grad_key.at[place]))
-        copies.append((dv.at[pair], grad_value.at[place]))
-    copies = [pltpu.make_async_copy(*one, sem.at[i]) for i, one in enumerate(copies)]
+def write_out(*refs):
+    sources, places, sem = refs[:3], refs[3:6], refs[6]
+    copies = [
+        pltpu.make_async_copy(source, place, sem.at[i])
+        for i, (source, place) in enumerate(zip(sources, places))
+    ]
     for copy in copies:
         copy.start()
     for copy in copies:
@@ -423,11 +444,7 @@
     wide = ROWS * 3
     parts = pl.pallas_call(
         functools.partial(kernel, n),
-        out_shape=[
-            pltpu.VMEM((CHUNKS, TILE, 128), BF16),
-            pltpu.VMEM((PAIRS, ROWS, 128), BF16),
-            pltpu.VMEM((PAIRS, ROWS, 128), BF16),
-        ],
+        out_shape=[pltpu.VMEM((rows, features), BF16)] * 3,
         in_specs=[far] * 6,
         out_specs=[near] * 3,
         scratch_shapes=[
@@ -436,8 +453,7 @@
             pltpu.VMEM((PAIRS, ROWS, 128), BF16),
             pltpu.VMEM((PAIRS, ROWS, 128), BF16),
             pltpu.VMEM((PAIRS, 128, ROWS), BF16),
-            pltpu.VMEM((PAIRS, wide, 128), BF16),
-            pltpu.VMEM((PAIRS, wide, 128), BF16),
+            pltpu.VMEM((PAIRS, 2, wide, 128), BF16),
             pltpu.VMEM((wide, 128), BF16),
             pltpu.VMEM((ROWS, 128), BF16),
             pltpu.VMEM((2, 8, 128), F32),
@@ -448,24 +464,21 @@
             pltpu.VMEM((RING, 2, 2, ROWS, TILE), F32),
             pltpu.VMEM((3, CHUNKS, 8, TILE), F32),
             pltpu.VMEM((2, CHUNKS, 2, 8, 128), F32),
-            pltpu.VMEM((2, CHUNKS, 2, 8, 128), F32),
-            pltpu.VMEM((2, CHUNKS, 8, 128), F32),
-            pltpu.VMEM((2, ROWS, wide), BF16),
-            pltpu.VMEM((2, ROWS, wide), BF16),
+            pltpu.VMEM((2, CHUNKS, 3, 8, 128), F32),
+            pltpu.VMEM((2 * ROWS, wide), BF16),
+            pltpu.VMEM((2 * ROWS, wide), BF16),
             pltpu.VMEM((CHUNKS, 128, TILE), F32),
             pltpu.VMEM((2, CHUNKS, 2, 64, TILE), BF16),
             pltpu.VMEM((2, CHUNKS, 2, 64, TILE), BF16),
-            dma((4 * PAIRS + 2,)),
-            dma((2, CHUNKS, 2)),
-            dma((2, CHUNKS, 2)),
+            dma((6,)),
+            dma((2,)),
+            dma((2, CHUNKS)),
+            dma((2,)),
             dma((2,)),
             dma((2,)),
             dma((2, CHUNKS)),
-            dma((2, CHUNKS)),
-            dma((2, CHUNKS)),
-            dma((2, CHUNKS)),
-            dma((2, CHUNKS, 2)),
-            dma((2, CHUNKS, 2)),
+            dma((2,)),
+            dma((2,)),
         ],
         compiler_params=pltpu.CompilerParams(
             collective_id=0, has_side_effects=True, vmem_limit_bytes=58 << 20
@@ -476,7 +489,7 @@
         out_shape=[out] * 3,
         in_specs=[near] * 3,
         out_specs=[far] * 3,
-        scratch_shapes=[dma((CHUNKS + 2 * PAIRS,))],
+        scratch_shapes=[dma((3,))],
     )(*[pltpu.with_memory_space_constraint(one, pltpu.VMEM) for one in parts])
 
 

time: 55.2 us -> 53.7 us (0.973)
  Pallas kernels: 54.5 us -> 53 us
    pallas_call x1, Pallas kernels: 53.2 us -> 51.8 us  [body(): pl.pallas_call(functools.partial(kernel, n), out_shape=[pltpu.VMEM((rows,...]
where the time goes in v4:
time: 53.7 us; the launch traced here: 53.6 us
  Pallas kernels  53 us (99%)
  between operations  0.64 us (1%)
    pallas_call x1, Pallas kernels, body(): pl.pallas_call(functools.partial(kernel, n), out_shape=[pltpu.VMEM((rows,...  51.8 us
    pallas_call x1, Pallas kernels, body(): pl.pallas_call(write_out, out_shape=[out] * 3, in_specs=[near] * 3, out_s...  1.17 us

profile of v4, /device:TPU:24, one launch (start us, length us, event | category | flops | bytes accessed | tf_op | source)
XLA Modules:
  0.0 53.6 jit_solution(14072370493338682705)
XLA Ops:
  0.6 51.8 %shard_map.85 = (bf16[512,512]{1,0:T(8,128)(2,1)S(1)}, bf16[512,512]{1,0:T(8,128)(2,1)S(1)}, bf16[512,512]{1,0:T(8,128)(2,1)S(1)}) custom-call(bf16[512,512]{1,0:T(8,128)(2,1)} %query.1, bf16[512,512]{1,0:T(8,128)(2,1)} %key.1, bf16[512,512]{1,0:T(8,128)(2,1)} %value.1, bf16[512,512]{1,0:T(8,128)(2,1)} %gout.1, s32[8,16]{1,0:T(8,128)} %neighbours.1, s32[1024]{0:T(1024)} %owner.1), custom_call_target="tpu_custom_call" | custom-call | tf_op jit(solution)/shard_map/pallas_call | solution.py:445
  52.5 1.2 %shard_map.86 = (bf16[512,512]{1,0:T(8,128)(2,1)}, bf16[512,512]{1,0:T(8,128)(2,1)}, bf16[512,512]{1,0:T(8,128)(2,1)}) custom-call(bf16[512,512]{1,0:T(8,128)(2,1)S(1)} %get-tuple-element.6.refs_0_, bf16[512,512]{1,0:T(8,128)(2,1)S(1)} %get-tuple-element.7.refs_1_, bf16[512,512]{1,0:T(8,128)(2,1)S(1)} %get-tuple-element.8.refs_2_), custom_call_target="tpu_custom_call" | custom-call | tf_op jit(solution)/shard_map/pallas_call | solution.py:487

commit v5 on v4

--- a/solution.py
+++ b/solution.py
@@ -17,7 +17,7 @@
 PAIRS = 4
 CHUNKS = PAIRS * ROWS // TILE
 RING = 4
-LAG_C, LAG_D = 3, 7
+LAG_C, LAG_D = 3, 8
 AHEAD = 3
 
 
@@ -381,9 +381,13 @@
             start(lambda flow: [stat_copy(s, flow)])
             start(lambda flow: [far_copy(s, flow)], far_sends)
 
-            @pl.when(s + AHEAD < CHUNKS)
+            @pl.when(s + AHEAD < CHUNKS - 1)
             def _():
                 start(bulk_copies(s + AHEAD))
+
+            @pl.when(s + AHEAD == CHUNKS - 2)
+            def _():
+                start(bulk_copies(CHUNKS - 1))
 
         @pl.when((s >= LAG_C) & (s < CHUNKS + LAG_C))
         def _():

time: 53.7 us -> 53.6 us (level)
  no operation moved by 1% of the time
where the time goes in v5:
time: 53.6 us; the launch traced here: 53.5 us
  Pallas kernels  52.9 us (99%)
  between operations  0.64 us (1%)
    pallas_call x1, Pallas kernels, body(): pl.pallas_call(functools.partial(kernel, n), out_shape=[pltpu.VMEM((rows,...  51.7 us
    pallas_call x1, Pallas kernels, body(): pl.pallas_call(write_out, out_shape=[out] * 3, in_specs=[near] * 3, out_s...  1.17 us

profile of v5, /device:TPU:24, one launch (start us, length us, event | category | flops | bytes accessed | tf_op | source)
XLA Modules:
  0.0 53.5 jit_solution(10262552842970076320)
XLA Ops:
  0.6 51.7 %shard_map.85 = (bf16[512,512]{1,0:T(8,128)(2,1)S(1)}, bf16[512,512]{1,0:T(8,128)(2,1)S(1)}, bf16[512,512]{1,0:T(8,128)(2,1)S(1)}) custom-call(bf16[512,512]{1,0:T(8,128)(2,1)} %query.1, bf16[512,512]{1,0:T(8,128)(2,1)} %key.1, bf16[512,512]{1,0:T(8,128)(2,1)} %value.1, bf16[512,512]{1,0:T(8,128)(2,1)} %gout.1, s32[8,16]{1,0:T(8,128)} %neighbours.1, s32[1024]{0:T(1024)} %owner.1), custom_call_target="tpu_custom_call" | custom-call | tf_op jit(solution)/shard_map/pallas_call | solution.py:449
  52.3 1.2 %shard_map.86 = (bf16[512,512]{1,0:T(8,128)(2,1)}, bf16[512,512]{1,0:T(8,128)(2,1)}, bf16[512,512]{1,0:T(8,128)(2,1)}) custom-call(bf16[512,512]{1,0:T(8,128)(2,1)S(1)} %get-tuple-element.6.refs_0_, bf16[512,512]{1,0:T(8,128)(2,1)S(1)} %get-tuple-element.7.refs_1_, bf16[512,512]{1,0:T(8,128)(2,1)S(1)} %get-tuple-element.8.refs_2_), custom_call_target="tpu_custom_call" | custom-call | tf_op jit(solution)/shard_map/pallas_call | solution.py:491
